TPU v7x, 128 devices: a whole 4x4x4 slice. The times are simulated.
128 devices in a mesh: region: 16 (over z_hi, y, core), member: 8 (over z_lo, x).
Axes of the slice: x: 4, y: 4, z: 4 (z_hi: 2, z_lo: 2; z = z_hi * 2 + z_lo), core: 2. Of those that a mesh axis runs over, the one named last changes fastest.
Arguments:
- controls: float32 [16, 8, 256, 512], P('member', None, 'region'), may hold values from -6 to 6
- perturbations: float32 [64, 8, 256, 512], P('member', None, 'region'), may hold values from -1.5 to 1.5
- assignment: int32 [64], replicated, may hold values from 0 to 15
- courant: float32 [4, 4, 8, 256, 512], P(None, None, 'member', 'region'), may hold values from 0.02 to 0.24
- innovation: float32 [8, 256, 512], P('member', 'region'), may hold values from -6 to 6
- obs_weight: float32 [8, 256, 512], P('member', 'region'), may hold values from 0.3 to 3
Outputs:
- gradient: float32 [16, 8, 256, 512], P('member', None, 'region')
- departure: float32 [8, 256, 512], P('member', 'region')
All inputs are finite; a program needn't handle non-finite values.
Results may differ from a plain program's by a relative error of at most 0.0001.
Values sent between devices are 32-bit elements; how exact they have to be, the bound alone decides.
A program may use at most 64 MiB of HBM per device.

v0:
```python
import functools

import jax
import jax.numpy as jnp
import numpy as np
from jax import lax
from jax.experimental import pallas as pl
from jax.experimental.pallas import tpu as pltpu
from jax.sharding import PartitionSpec as P

PASSES = 16
STEPS = 4
GROUP = 8
HALO = 8
MESH = pl.DeviceIdType.MESH
F32 = jnp.float32
BF16 = jnp.bfloat16


def tables(columns):
    index = np.arange(1, columns + 1, dtype=np.float64)
    sine = np.sqrt(2.0 / (columns + 1)) * np.sin(np.pi * np.outer(index, index) / (columns + 1))
    high = sine.astype(BF16)
    low = (sine - high.astype(np.float64)).astype(BF16)
    center = (1.0 + 2.0 * np.cos(np.pi * index / (columns + 1))) / 5.0
    power = np.ones((1, columns))
    for _ in range(PASSES):
        wider = np.zeros((power.shape[0] + 2, columns))
        wider[1:-1] += center * power
        wider[2:] += power / 5.0
        wider[:-2] += power / 5.0
        power = wider
    coef = np.broadcast_to(power[PASSES:, None, :], (PASSES + 1, GROUP, columns))
    return high, low, np.ascontiguousarray(coef).astype(np.float32)


def split(x):
    high = x.astype(BF16)
    return high, (x - high.astype(F32)).astype(BF16)


def times_sine(x, vhi, vlo):
    high, low = split(x)
    out = jnp.dot(high, vhi[...], preferred_element_type=F32)
    out += jnp.dot(low, vhi[...], preferred_element_type=F32)
    out += jnp.dot(high, vlo[...], preferred_element_type=F32)
    return out


def kernel(
    regions, ctl, pert, assign, cour, innov, weight, vhi_in, vlo_in, coef_in,
    lft, dep_out,
    vhi, vlo, coef, ctl3, pbuf, smo_out, smo, ms, inc, cour_x, inn_x, wgt_x, adj, dep, modes, rows, mid, fin,
    load_sem, pert_send, pert_recv, nb_send, nb_recv, smo_send, smo_recv, fin_send, fin_recv, out_sem,
):
    r, me = lax.axis_index("region"), lax.axis_index("member")
    fl, levels, height, columns = ctl.shape
    kl = pert.shape[0]
    fields = fl * levels
    groups = fields // GROUP
    last = regions - 1

    barrier = pltpu.get_barrier_semaphore()

    def peer(d):
        return lax.rem(me + d, levels)

    for d in range(1, levels):
        pl.semaphore_signal(barrier, inc=1, device_id=(r, peer(d)), device_id_type=MESH)

    @pl.when(r > 0)
    def _():
        pl.semaphore_signal(barrier, inc=1, device_id=(r - 1, me), device_id_type=MESH)

    @pl.when(r < last)
    def _():
        pl.semaphore_signal(barrier, inc=1, device_id=(r + 1, me), device_id_type=MESH)

    loads = [
        pltpu.make_async_copy(vhi_in, vhi, load_sem.at[0]),
        pltpu.make_async_copy(vlo_in, vlo, load_sem.at[1]),
        pltpu.make_async_copy(coef_in, coef, load_sem.at[2]),
        pltpu.make_async_copy(ctl, ctl3.at[1], load_sem.at[3]),
        pltpu.make_async_copy(pert.at[:, me], pbuf.at[pl.ds(me * kl, kl)], load_sem.at[4]),
        pltpu.make_async_copy(cour.at[:, :, 0], cour_x.at[:, :, pl.ds(HALO, height)], load_sem.at[5]),
        pltpu.make_async_copy(innov.at[0], inn_x.at[pl.ds(HALO, height)], load_sem.at[6]),
        pltpu.make_async_copy(weight.at[0], wgt_x.at[pl.ds(HALO, height)], load_sem.at[7]),
    ]
    for copy in loads:
        copy.start()

    top, bottom = pl.ds(0, HALO), pl.ds(height - HALO, HALO)
    above, below = pl.ds(0, HALO), pl.ds(HALO + height, HALO)
    nb = [
        ((ctl, ctl3.at[0]), (ctl, ctl3.at[2])),
        ((cour.at[:, :, 0, bottom], cour_x.at[:, :, above]), (cour.at[:, :, 0, top], cour_x.at[:, :, below])),
        ((innov.at[0, bottom], inn_x.at[above]), (innov.at[0, top], inn_x.at[below])),
        ((weight.at[0, bottom], wgt_x.at[above]), (weight.at[0, top], wgt_x.at[below])),
        ((ms.at[1], ms.at[0]), (ms.at[1], ms.at[2])),
        ((inc.at[pl.ds(height, HALO)], inc.at[above]), (inc.at[pl.ds(HALO, HALO)], inc.at[below])),
        ((adj.at[1], adj.at[0]), (adj.at[1], adj.at[2])),
    ]

    def to_neighbour(number, up):
        src, dst = nb[number][up]
        return pltpu.make_async_remote_copy(
            src_ref=src, dst_ref=dst, send_sem=nb_send.at[number, up], recv_sem=nb_recv.at[number, up],
            device_id=(r - 1 if up else r + 1, me), device_id_type=MESH,
        )

    def exchange(number):
        @pl.when(r < last)
        def _():
            to_neighbour(number, 0).start()

        @pl.when(r > 0)
        def _():
            to_neighbour(number, 1).start()

    def arrived(number):
        @pl.when(r > 0)
        def _():
            to_neighbour(number, 0).wait_recv()

        @pl.when(r < last)
        def _():
            to_neighbour(number, 1).wait_recv()

    def sent(number):
        @pl.when(r < last)
        def _():
            to_neighbour(number, 0).wait_send()

        @pl.when(r > 0)
        def _():
            to_neighbour(number, 1).wait_send()

    def pert_copy(to, source):
        return pltpu.make_async_remote_copy(
            src_ref=pert.at[:, to], dst_ref=pbuf.at[pl.ds(source * kl, kl)],
            send_sem=pert_send.at[to], recv_sem=pert_recv.at[source],
            device_id=(r, to), device_id_type=MESH,
        )

    neighbours = (r > 0).astype(jnp.int32) + (r < last).astype(jnp.int32)
    pl.semaphore_wait(barrier, levels - 1 + neighbours)

    exchange(0)
    for d in range(1, levels):
        pert_copy(peer(d), me).start()
    for number in (1, 2, 3):
        exchange(number)

    @pl.when(r == 0)
    def _():
        for ref in (inn_x, wgt_x, inc):
            ref[0:HALO] = jnp.zeros((HALO, columns), F32)
        cour_x[:, :, 0:HALO] = jnp.zeros((STEPS, 4, HALO, columns), F32)

    @pl.when(r == last)
    def _():
        for ref in (inn_x, wgt_x, inc):
            ref[HALO + height :] = jnp.zeros((HALO, columns), F32)
        cour_x[:, :, HALO + height :] = jnp.zeros((STEPS, 4, HALO, columns), F32)

    def smooth(x, keep):
        flat = jnp.concatenate([part.reshape(GROUP * height, columns) for part in x], axis=0)
        spectrum = times_sine(flat, vhi, vlo)
        for t in range(columns // 128):
            lane = slice(t * 128, (t + 1) * 128)
            modes[t] = spectrum[:, lane]
            for part in range(3):
                for i in range(height):
                    rows[part * height + i, :, lane] = modes[t, pl.ds(part * GROUP * height + i, GROUP, stride=height), :]

        @pl.when(r == 0)
        def _():
            rows[height - 1] = jnp.zeros((GROUP, columns), F32)
            for k in range(1, height):
                rows[height - 1 - k] = -rows[height - 1 + k]

        @pl.when(r == last)
        def _():
            rows[2 * height] = jnp.zeros((GROUP, columns), F32)
            for k in range(1, height):
                rows[2 * height + k] = -rows[2 * height - k]

        step = 4
        tiles = columns // 128

        @pl.loop(0, tiles * (height // step))
        def _(it):
            t = lax.rem(it, tiles)
            lane = pl.ds(pl.multiple_of(t * 128, 128), 128)
            i = (it // tiles) * step
            g = [rows[i + j, :, lane] for j in range(2 * PASSES + step)]
            total = [None] * step
            for d in range(PASSES + 1):
                c = coef[d, :, lane]
                for j in range(step):
                    at = PASSES + j
                    term = c * g[at] if d == 0 else c * (g[at - d] + g[at + d])
                    total[j] = term if d == 0 else total[j] + term
            for j in range(step):
                mid[t, pl.ds(i + j, GROUP, stride=height), :] = total[j]

        keep(times_sine(jnp.concatenate([mid[t] for t in range(tiles)], axis=1), vhi, vlo))

    for number in (0, 1, 2, 3):
        loads[number].wait()
    arrived(0)

    def smo_copy(plane, field, level, source):
        return pltpu.make_async_remote_copy(
            src_ref=smo_out.at[plane], dst_ref=smo.at[source * fl + field],
            send_sem=smo_send.at[plane], recv_sem=smo_recv.at[source, field],
            device_id=(r, level), device_id_type=MESH,
        )

    def smo_own(plane, field):
        return pltpu.make_async_copy(smo_out.at[plane], smo.at[me * fl + field], smo_send.at[plane])

    for q in range(groups):
        parts = [
            jnp.concatenate([ctl3[part, (q * GROUP + j) // levels, (q * GROUP + j) % levels][None] for j in range(GROUP)])
            for part in range(3)
        ]

        def keep(result, q=q):
            smo_out[q * GROUP : (q + 1) * GROUP] = result.reshape(GROUP, height, columns)

        smooth(parts, keep)
        for j in range(GROUP):
            plane = q * GROUP + j
            field, level = plane // levels, plane % levels

            @pl.when(me != level)
            def _():
                smo_copy(plane, field, level, me).start()

            @pl.when(me == level)
            def _():
                smo_own(plane, field).start()

    loads[4].wait()
    tiles = columns // 128

    def add_source(source, first):
        which = [assign[source * kl + k] for k in range(kl)]

        @pl.loop(0, (height // 8) * tiles)
        def _(it):
            lane = pl.ds(pl.multiple_of(lax.rem(it, tiles) * 128, 128), 128)
            row = pl.ds(pl.multiple_of((it // tiles) * 8, 8), 8)
            p = [pbuf[source * kl + k, row, lane] for k in range(kl)]
            for l in range(fields):
                terms = [jnp.where(which[k] == l, 1.0, 0.0) * p[k] for k in range(kl)]
                while len(terms) > 1:
                    terms = [a + b for a, b in zip(terms[::2], terms[1::2])]
                ms[1, l, row, lane] = terms[0] if first else ms[1, l, row, lane] + terms[0]

    add_source(me, True)
    for d in range(1, levels):
        source = peer(levels - d)
        pert_copy(source, source).wait_recv()
        add_source(source, False)
    exchange(4)

    for d in range(levels):
        source = peer(d)
        for field in range(fl):
            if d == 0:
                smo_own(field * levels + me, field).wait()
            else:
                smo_copy(field * levels + me, field, me, source).wait_recv()

    total = smo[0] * ms[1, 0]
    for l in range(1, fields):
        total += smo[l] * ms[1, l]
    inc[HALO : HALO + height] = total
    exchange(5)
    for number in (5, 6, 7):
        loads[number].wait()
    for number in (1, 2, 3, 5):
        arrived(number)

    extent = height + 2 * HALO
    column = lax.broadcasted_iota(jnp.int32, (extent, columns), 1)

    def from_west(y):
        return jnp.where(column == 0, 0.0, pltpu.roll(y, 1, 1))

    def from_east(y):
        return jnp.where(column == columns - 1, 0.0, pltpu.roll(y, columns - 1, 1))

    def from_north(y):
        return pltpu.roll(y, 1, 0)

    def from_south(y):
        return pltpu.roll(y, extent - 1, 0)

    state = inc[...]
    for s in range(STEPS):
        n, so, w, e = (cour_x[s, k] for k in range(4))
        state = (
            (1.0 - (n + so + w + e)) * state
            + n * from_north(state) + so * from_south(state) + w * from_west(state) + e * from_east(state)
        )
    state = wgt_x[...] * (state - inn_x[...])
    dep[...] = state[HALO : HALO + height]
    dep_copy = pltpu.make_async_copy(dep, dep_out.at[0], out_sem)
    dep_copy.start()
    for s in range(STEPS - 1, -1, -1):
        n, so, w, e = (cour_x[s, k] for k in range(4))
        state = (
            (1.0 - (n + so + w + e)) * state
            + from_south(n * state) + from_north(so * state) + from_east(w * state) + from_west(e * state)
        )
    adj[1] = state[HALO : HALO + height]
    exchange(6)
    arrived(4)
    arrived(6)

    def fin_copy(owner, level):
        return pltpu.make_async_remote_copy(
            src_ref=fin.at[pl.ds(owner * fl, fl)], dst_ref=lft.at[:, level],
            send_sem=fin_send.at[owner], recv_sem=fin_recv.at[level],
            device_id=(r, owner), device_id_type=MESH,
        )

    def fin_own():
        return pltpu.make_async_copy(fin.at[pl.ds(me * fl, fl)], lft.at[:, me], fin_send.at[me])

    for q in range(groups):
        parts = [ms[part, q * GROUP : (q + 1) * GROUP] * adj[part][None] for part in range(3)]

        def keep(result, q=q):
            fin[q * GROUP : (q + 1) * GROUP] = result.reshape(GROUP, height, columns)

        smooth(parts, keep)
        for owner in range(q * GROUP // fl, (q + 1) * GROUP // fl):
            @pl.when(me != owner)
            def _():
                fin_copy(owner, me).start()

            @pl.when(me == owner)
            def _():
                fin_own().start()

    for d in range(1, levels):
        pert_copy(peer(d), me).wait_send()
    for plane in range(fl * levels):
        @pl.when(me != plane % levels)
        def _():
            smo_copy(plane, plane // levels, plane % levels, me).wait_send()
    for number in range(len(nb)):
        sent(number)
    dep_copy.wait()
    fin_own().wait()
    for d in range(1, levels):
        fin_copy(peer(d), me).wait_send()
    for d in range(1, levels):
        fin_copy(me, peer(d)).wait_recv()


def solution(mesh):
    regions = mesh.shape["region"]

    def shards(controls, perturbations, assignment, courant, innovation, obs_weight):
        fl, levels, height, columns = controls.shape
        kl = perturbations.shape[0]
        fields = fl * levels
        vhi, vlo, coef = tables(columns)
        extent = height + 2 * HALO
        any_space = pl.BlockSpec(memory_space=pl.ANY)
        smem = pl.BlockSpec(memory_space=pltpu.SMEM)
        dma = pltpu.SemaphoreType.DMA
        lft, departure = pl.pallas_call(
            functools.partial(kernel, regions),
            out_shape=(
                jax.ShapeDtypeStruct(controls.shape, F32),
                jax.ShapeDtypeStruct(innovation.shape, F32),
            ),
            in_specs=[any_space, any_space, smem] + [any_space] * 6,
            out_specs=(any_space, any_space),
            scratch_shapes=[
                pltpu.VMEM((columns, columns), BF16),
                pltpu.VMEM((columns, columns), BF16),
                pltpu.VMEM((PASSES + 1, GROUP, columns), F32),
                pltpu.VMEM((3, fl, levels, height, columns), F32),
                pltpu.VMEM((kl * levels, height, columns), F32),
                pltpu.VMEM((fields, height, columns), F32),
                pltpu.VMEM((fields, height, columns), F32),
                pltpu.VMEM((3, fields, height, columns), F32),
                pltpu.VMEM((extent, columns), F32),
                pltpu.VMEM((STEPS, 4, extent, columns), F32),
                pltpu.VMEM((extent, columns), F32),
                pltpu.VMEM((extent, columns), F32),
                pltpu.VMEM((3, height, columns), F32),
                pltpu.VMEM((height, columns), F32),
                pltpu.VMEM((columns // 128, 3 * GROUP * height, 128), F32),
                pltpu.VMEM((3 * height, GROUP, columns), F32),
                pltpu.VMEM((columns // 128, GROUP * height, 128), F32),
                pltpu.VMEM((fields, height, columns), F32),
                dma((8,)),
                dma((levels,)),
                dma((levels,)),
                dma((7, 2)),
                dma((7, 2)),
                dma((fields,)),
                dma((levels, fl)),
                dma((levels,)),
                dma((levels,)),
                dma,
            ],
            compiler_params=pltpu.CompilerParams(
                collective_id=0, has_side_effects=True, vmem_limit_bytes=40 * 2**20
            ),
            cost_estimate=pl.CostEstimate(flops=2 * 10**9, bytes_accessed=8 * 2**20, transcendentals=0),
        )(controls, perturbations, assignment, courant, innovation, obs_weight, vhi, vlo, coef)
        return controls + lft, departure

    return jax.shard_map(
        shards,
        mesh=mesh,
        in_specs=(
            P("member", None, "region", None),
            P("member", None, "region", None),
            P(),
            P(None, None, "member", "region", None),
            P("member", "region", None),
            P("member", "region", None),
        ),
        out_specs=(P("member", None, "region", None), P("member", "region", None)),
        check_vma=False,
    )
```

profile of v0, /device:TPU:120, one launch (start us, length us, event | category | flops | bytes accessed | tf_op | source)
XLA Modules:
  0.0 82.6 jit_solution(6276434397908312960)
XLA Ops:
  0.6 0.0 copy-start
  0.6 1.0 %copy-done = f32[2,8,16,512]{3,2,1,0:T(8,128)S(1)} copy-done((f32[2,8,16,512]{3,2,1,0:T(8,128)S(1)}, f32[2,8,16,512]{3,2,1,0:T(8,128)}, u32[]{:S(2)}) %copy-start) | copy-done | bytes 524312
  1.7 0.0 copy-start.1
  1.7 1.6 %copy-done.1 = f32[8,8,16,512]{3,2,1,0:T(8,128)S(1)} copy-done((f32[8,8,16,512]{3,2,1,0:T(8,128)S(1)}, f32[8,8,16,512]{3,2,1,0:T(8,128)}, u32[]{:S(2)}) %copy-start.1) | copy-done | bytes 2097176
  3.3 0.0 copy-start.2
  3.3 1.0 %copy-done.2 = f32[4,4,1,16,512]{4,3,2,1,0:T(8,128)S(1)} copy-done((f32[4,4,1,16,512]{4,3,2,1,0:T(8,128)S(1)}, f32[4,4,1,16,512]{4,3,2,1,0:T(8,128)}, u32[]{:S(2)}) %copy-start.2) | copy-done | bytes 524312
  4.3 0.0 copy-start.3
  4.3 0.8 copy-done.3
  5.1 0.0 copy-start.4
  5.1 0.8 copy-done.4
  5.8 0.0 copy-start.5
  5.8 0.7 copy-done.5
  6.5 0.0 copy-start.6
  6.5 1.0 %copy-done.6 = bf16[512,512]{1,0:T(8,128)(2,1)S(1)} copy-done((bf16[512,512]{1,0:T(8,128)(2,1)S(1)}, bf16[512,512]{1,0:T(8,128)(2,1)}, u32[]{:S(2)}) %copy-start.6) | copy-done | bytes 524312
  7.5 0.0 copy-start.7
  7.5 1.0 %copy-done.7 = bf16[512,512]{1,0:T(8,128)(2,1)S(1)} copy-done((bf16[512,512]{1,0:T(8,128)(2,1)S(1)}, bf16[512,512]{1,0:T(8,128)(2,1)}, u32[]{:S(2)}) %copy-start.7) | copy-done | bytes 524312
  8.6 0.0 copy-start.8
  8.6 1.0 %copy-done.8 = f32[17,8,512]{2,1,0:T(8,128)S(1)} copy-done((f32[17,8,512]{2,1,0:T(8,128)S(1)}, f32[17,8,512]{2,1,0:T(8,128)}, u32[]{:S(2)}) %copy-start.8) | copy-done | bytes 278552
  9.5 71.6 %shard_map.104 = (f32[2,8,16,512]{3,2,1,0:T(8,128)S(1)}, f32[1,16,512]{2,1,0:T(8,128)S(1)}) custom-call(f32[2,8,16,512]{3,2,1,0:T(8,128)S(1)} %copy-done, f32[8,8,16,512]{3,2,1,0:T(8,128)S(1)} %copy-done.1, s32[64]{0:T(128)S(1)} %copy-done.5, f32[4,4,1,16,512]{4,3,2,1,0:T(8,128)S(1)} %copy-done.2, f32[1,16,512]{2,1,0:T(8,128)S(1)} %copy-done.3, ...), custom_call_target="tpu_custom_call" | custom-call | flops 2000000000 | bytes 8388608 | tf_op jit(solution)/shard_map/pallas_call | solution.py:378
  81.1 0.9 %add.3 = f32[2,8,16,512]{3,2,1,0:T(8,128)} add(f32[2,8,16,512]{3,2,1,0:T(8,128)S(1)} %copy-done, f32[2,8,16,512]{3,2,1,0:T(8,128)S(1)} %get-tuple-element.4) | non-fusion elementwise | flops 131072 | bytes 1572864 | tf_op jit(solution)/shard_map/add | solution.py:421
  82.0 0.6 copy.12
Async XLA Ops:
  0.6 1.0 %copy-start = (f32[2,8,16,512]{3,2,1,0:T(8,128)S(1)}, f32[2,8,16,512]{3,2,1,0:T(8,128)}, u32[]{:S(2)}) copy-start(f32[2,8,16,512]{3,2,1,0:T(8,128)} %ctl.1) | copy-start | bytes 1572868
  1.7 1.6 %copy-start.1 = (f32[8,8,16,512]{3,2,1,0:T(8,128)S(1)}, f32[8,8,16,512]{3,2,1,0:T(8,128)}, u32[]{:S(2)}) copy-start(f32[8,8,16,512]{3,2,1,0:T(8,128)} %pert.1) | copy-start | bytes 6291460
  3.3 1.0 %copy-start.2 = (f32[4,4,1,16,512]{4,3,2,1,0:T(8,128)S(1)}, f32[4,4,1,16,512]{4,3,2,1,0:T(8,128)}, u32[]{:S(2)}) copy-start(f32[4,4,1,16,512]{4,3,2,1,0:T(8,128)} %cour.1) | copy-start | bytes 1572868
  4.3 0.8 copy-start.3
  5.1 0.8 copy-start.4
  5.8 0.7 copy-start.5
  6.5 1.0 %copy-start.6 = (bf16[512,512]{1,0:T(8,128)(2,1)S(1)}, bf16[512,512]{1,0:T(8,128)(2,1)}, u32[]{:S(2)}) copy-start(bf16[512,512]{1,0:T(8,128)(2,1)} %constant.7.clone.vlo_in) | copy-start | bytes 1572868
  7.5 1.0 %copy-start.7 = (bf16[512,512]{1,0:T(8,128)(2,1)S(1)}, bf16[512,512]{1,0:T(8,128)(2,1)}, u32[]{:S(2)}) copy-start(bf16[512,512]{1,0:T(8,128)(2,1)} %constant.6.clone.vhi_in) | copy-start | bytes 1572868
  8.6 1.0 %copy-start.8 = (f32[17,8,512]{2,1,0:T(8,128)S(1)}, f32[17,8,512]{2,1,0:T(8,128)}, u32[]{:S(2)}) copy-start(f32[17,8,512]{2,1,0:T(8,128)} %constant.8.clone.coef_in) | copy-start | bytes 835588
where the time goes:
time: 83.1 us; the launch traced here: 82.6 us
  Pallas kernels  71.6 us (86%)
  local copies, waits for them, and re-layouts  9.49 us (11%)
  other arithmetic  0.88 us (1%)
    pallas_call x1, Pallas kernels, shards(): pl.pallas_call(functools.partial(kernel, regions), out_shape=(jax.ShapeDt...  71.6 us
    unnamed x19, local copies, waits for them, and re-layouts  9.49 us

commit v1 on v0

--- a/solution.py
+++ b/solution.py
@@ -13,6 +13,7 @@
 GROUP = 8
 HALO = 8
 MESH = pl.DeviceIdType.MESH
+ORDER = ((1, 1), (3, 0), (2, 1), (0, 1), (2, 0), (3, 1), (1, 0))
 F32 = jnp.float32
 BF16 = jnp.bfloat16
 
@@ -62,11 +63,17 @@
 
     barrier = pltpu.get_barrier_semaphore()
 
-    def peer(d):
-        return lax.rem(me + d, levels)
-
-    for d in range(1, levels):
-        pl.semaphore_signal(barrier, inc=1, device_id=(r, peer(d)), device_id_type=MESH)
+    xs = levels // 2
+    order = [offset for offset in ORDER if offset[0] < xs]
+    mx, mz = lax.rem(me, xs), me // xs
+
+    def member(x, z):
+        return lax.rem(mz + z, 2) * xs + lax.rem(mx + x, xs)
+
+    targets = [member(x, z) for x, z in order]
+    sources = [member(xs - x, z) for x, z in order]
+    for to in targets:
+        pl.semaphore_signal(barrier, inc=1, device_id=(r, to), device_id_type=MESH)
 
     @pl.when(r > 0)
     def _():
@@ -96,9 +103,10 @@
         ((cour.at[:, :, 0, bottom], cour_x.at[:, :, above]), (cour.at[:, :, 0, top], cour_x.at[:, :, below])),
         ((innov.at[0, bottom], inn_x.at[above]), (innov.at[0, top], inn_x.at[below])),
         ((weight.at[0, bottom], wgt_x.at[above]), (weight.at[0, top], wgt_x.at[below])),
-        ((ms.at[1], ms.at[0]), (ms.at[1], ms.at[2])),
+        ((ms.at[1, :, top], ms.at[0, :, top]), (ms.at[1, :, top], ms.at[2, :, top])),
         ((inc.at[pl.ds(height, HALO)], inc.at[above]), (inc.at[pl.ds(HALO, HALO)], inc.at[below])),
         ((adj.at[1], adj.at[0]), (adj.at[1], adj.at[2])),
+        ((ms.at[1, :, bottom], ms.at[0, :, bottom]), (ms.at[1, :, bottom], ms.at[2, :, bottom])),
     ]
 
     def to_neighbour(number, up):
@@ -135,10 +143,12 @@
         def _():
             to_neighbour(number, 1).wait_send()
 
-    def pert_copy(to, source):
+    halves = (top, bottom)
+
+    def pert_copy(to, source, half):
         return pltpu.make_async_remote_copy(
-            src_ref=pert.at[:, to], dst_ref=pbuf.at[pl.ds(source * kl, kl)],
-            send_sem=pert_send.at[to], recv_sem=pert_recv.at[source],
+            src_ref=pert.at[:, to, halves[half]], dst_ref=pbuf.at[pl.ds(source * kl, kl), halves[half]],
+            send_sem=pert_send.at[to, half], recv_sem=pert_recv.at[source, half],
             device_id=(r, to), device_id_type=MESH,
         )
 
@@ -146,8 +156,9 @@
     pl.semaphore_wait(barrier, levels - 1 + neighbours)
 
     exchange(0)
-    for d in range(1, levels):
-        pert_copy(peer(d), me).start()
+    for half in range(2):
+        for to in targets:
+            pert_copy(to, me, half).start()
     for number in (1, 2, 3):
         exchange(number)
 
@@ -206,6 +217,19 @@
 
         keep(times_sine(jnp.concatenate([mid[t] for t in range(tiles)], axis=1), vhi, vlo))
 
+    def add_source(source, half, first):
+        which = [assign[source * kl + k] for k in range(kl)]
+        p = [pbuf[source * kl + k, halves[half]] for k in range(kl)]
+        for l in range(fields):
+            terms = [jnp.where(which[k] == l, 1.0, 0.0) * p[k] for k in range(kl)]
+            while len(terms) > 1:
+                terms = [a + b for a, b in zip(terms[::2], terms[1::2])]
+            ms[1, l, halves[half]] = terms[0] if first else ms[1, l, halves[half]] + terms[0]
+
+    loads[4].wait()
+    for half in range(2):
+        add_source(me, half, True)
+
     for number in (0, 1, 2, 3):
         loads[number].wait()
     arrived(0)
@@ -230,49 +254,21 @@
             smo_out[q * GROUP : (q + 1) * GROUP] = result.reshape(GROUP, height, columns)
 
         smooth(parts, keep)
-        for j in range(GROUP):
-            plane = q * GROUP + j
-            field, level = plane // levels, plane % levels
-
-            @pl.when(me != level)
-            def _():
-                smo_copy(plane, field, level, me).start()
-
-            @pl.when(me == level)
-            def _():
-                smo_own(plane, field).start()
-
-    loads[4].wait()
-    tiles = columns // 128
-
-    def add_source(source, first):
-        which = [assign[source * kl + k] for k in range(kl)]
-
-        @pl.loop(0, (height // 8) * tiles)
-        def _(it):
-            lane = pl.ds(pl.multiple_of(lax.rem(it, tiles) * 128, 128), 128)
-            row = pl.ds(pl.multiple_of((it // tiles) * 8, 8), 8)
-            p = [pbuf[source * kl + k, row, lane] for k in range(kl)]
-            for l in range(fields):
-                terms = [jnp.where(which[k] == l, 1.0, 0.0) * p[k] for k in range(kl)]
-                while len(terms) > 1:
-                    terms = [a + b for a, b in zip(terms[::2], terms[1::2])]
-                ms[1, l, row, lane] = terms[0] if first else ms[1, l, row, lane] + terms[0]
-
-    add_source(me, True)
-    for d in range(1, levels):
-        source = peer(levels - d)
-        pert_copy(source, source).wait_recv()
-        add_source(source, False)
-    exchange(4)
-
-    for d in range(levels):
-        source = peer(d)
-        for field in range(fl):
-            if d == 0:
-                smo_own(field * levels + me, field).wait()
-            else:
-                smo_copy(field * levels + me, field, me, source).wait_recv()
+        for field in range(q * GROUP // levels, (q + 1) * GROUP // levels):
+            for to in targets:
+                smo_copy(field * levels + to, field, to, me).start()
+            smo_own(field * levels + me, field).start()
+
+    for half in range(2):
+        for source in sources:
+            pert_copy(source, source, half).wait_recv()
+            add_source(source, half, False)
+        exchange((4, 7)[half])
+
+    for field in range(fl):
+        smo_own(field * levels + me, field).wait()
+        for source in sources:
+            smo_copy(field * levels + me, field, me, source).wait_recv()
 
     total = smo[0] * ms[1, 0]
     for l in range(1, fields):
@@ -318,8 +314,8 @@
         )
     adj[1] = state[HALO : HALO + height]
     exchange(6)
-    arrived(4)
-    arrived(6)
+    for number in (4, 7, 6):
+        arrived(number)
 
     def fin_copy(owner, level):
         return pltpu.make_async_remote_copy(
@@ -332,35 +328,32 @@
         return pltpu.make_async_copy(fin.at[pl.ds(me * fl, fl)], lft.at[:, me], fin_send.at[me])
 
     for q in range(groups):
-        parts = [ms[part, q * GROUP : (q + 1) * GROUP] * adj[part][None] for part in range(3)]
-
-        def keep(result, q=q):
-            fin[q * GROUP : (q + 1) * GROUP] = result.reshape(GROUP, height, columns)
+        begin = lax.rem(mz + 1 + q, 2) * GROUP if groups == 2 else q * GROUP
+        parts = [ms[part, pl.ds(begin, GROUP)] * adj[part][None] for part in range(3)]
+
+        def keep(result, begin=begin):
+            fin[pl.ds(begin, GROUP)] = result.reshape(GROUP, height, columns)
 
         smooth(parts, keep)
-        for owner in range(q * GROUP // fl, (q + 1) * GROUP // fl):
-            @pl.when(me != owner)
-            def _():
-                fin_copy(owner, me).start()
-
-            @pl.when(me == owner)
-            def _():
-                fin_own().start()
-
-    for d in range(1, levels):
-        pert_copy(peer(d), me).wait_send()
-    for plane in range(fl * levels):
-        @pl.when(me != plane % levels)
-        def _():
-            smo_copy(plane, plane // levels, plane % levels, me).wait_send()
+        for (x, z), to in zip(order, targets):
+            if groups == 1 or z == 1 - q:
+                fin_copy(to, me).start()
+        if q == groups - 1:
+            fin_own().start()
+
+    for to in targets:
+        for half in range(2):
+            pert_copy(to, me, half).wait_send()
+        for field in range(fl):
+            smo_copy(field * levels + to, field, to, me).wait_send()
     for number in range(len(nb)):
         sent(number)
     dep_copy.wait()
     fin_own().wait()
-    for d in range(1, levels):
-        fin_copy(peer(d), me).wait_send()
-    for d in range(1, levels):
-        fin_copy(me, peer(d)).wait_recv()
+    for to in targets:
+        fin_copy(to, me).wait_send()
+    for source in sources:
+        fin_copy(me, source).wait_recv()
 
 
 def solution(mesh):
@@ -372,7 +365,7 @@
         fields = fl * levels
         vhi, vlo, coef = tables(columns)
         extent = height + 2 * HALO
-        any_space = pl.BlockSpec(memory_space=pl.ANY)
+        any_space = pl.BlockSpec(memory_space=pltpu.HBM)
         smem = pl.BlockSpec(memory_space=pltpu.SMEM)
         dma = pltpu.SemaphoreType.DMA
         lft, departure = pl.pallas_call(
@@ -403,10 +396,10 @@
                 pltpu.VMEM((columns // 128, GROUP * height, 128), F32),
                 pltpu.VMEM((fields, height, columns), F32),
                 dma((8,)),
-                dma((levels,)),
-                dma((levels,)),
-                dma((7, 2)),
-                dma((7, 2)),
+                dma((levels, 2)),
+                dma((levels, 2)),
+                dma((8, 2)),
+                dma((8, 2)),
                 dma((fields,)),
                 dma((levels, fl)),
                 dma((levels,)),
@@ -414,7 +407,7 @@
                 dma,
             ],
             compiler_params=pltpu.CompilerParams(
-                collective_id=0, has_side_effects=True, vmem_limit_bytes=40 * 2**20
+                collective_id=0, has_side_effects=True, vmem_limit_bytes=56 * 2**20
             ),
             cost_estimate=pl.CostEstimate(flops=2 * 10**9, bytes_accessed=8 * 2**20, transcendentals=0),
         )(controls, perturbations, assignment, courant, innovation, obs_weight, vhi, vlo, coef)

time: 83.1 us -> 72.2 us (0.87)
  the two profiles are of different devices: /device:TPU:120 before, /device:TPU:1 now
where the time goes in v1:
time: 72.2 us; the launch traced here: 72 us
  Pallas kernels  68 us (94%)
  other arithmetic  1.93 us (3%)
  local copies, waits for them, and re-layouts  1.38 us (2%)
    pallas_call x1, Pallas kernels, shards(): pl.pallas_call(functools.partial(kernel, regions), out_shape=(jax.ShapeDt...  68 us
    add x1, other arithmetic, shards(): return (controls + lft, departure)  1.93 us

profile of v1, /device:TPU:1, one launch (start us, length us, event | category | flops | bytes accessed | tf_op | source)
XLA Modules:
  0.0 72.0 jit_solution(15643265932069176690)
XLA Ops:
  0.6 0.0 copy-start
  0.6 68.0 %shard_map.104 = (f32[2,8,16,512]{3,2,1,0:T(8,128)}, f32[1,16,512]{2,1,0:T(8,128)}) custom-call(f32[2,8,16,512]{3,2,1,0:T(8,128)} %ctl.1, f32[8,8,16,512]{3,2,1,0:T(8,128)} %pert.1, s32[64]{0:T(128)} %assign.1, f32[4,4,1,16,512]{4,3,2,1,0:T(8,128)} %cour.1, f32[1,16,512]{2,1,0:T(8,128)} %innov.1, f32[1,16,512]{2,1,0:T(8,128)} %weight.1, ...), custom_call_target="tpu_custom_call" | custom-call | flops 2000000000 | bytes 8388608 | tf_op jit(solution)/shard_map/pallas_call | solution.py:371
  68.6 0.0 copy-done
  68.7 1.9 %add.3 = f32[2,8,16,512]{3,2,1,0:T(8,128)} add(f32[2,8,16,512]{3,2,1,0:T(8,128)S(1)} %copy-done, f32[2,8,16,512]{3,2,1,0:T(8,128)} %get-tuple-element.4) | non-fusion elementwise | flops 131072 | bytes 1572864 | tf_op jit(solution)/shard_map/add | solution.py:414
  70.6 1.4 %copy.12 = f32[1,16,512]{2,1,0:T(8,128)} copy(f32[1,16,512]{2,1,0:T(8,128)} %get-tuple-element.9) | data formatting | bytes 65536
Async XLA Ops:
  0.6 68.0 %copy-start = (f32[2,8,16,512]{3,2,1,0:T(8,128)S(1)}, f32[2,8,16,512]{3,2,1,0:T(8,128)}, u32[]{:S(2)}) copy-start(f32[2,8,16,512]{3,2,1,0:T(8,128)} %ctl.1) | copy-start | bytes 1572868

commit v2 on v1

v2 whole, which is shorter than its diff:
```python
import functools

import jax
import jax.numpy as jnp
import numpy as np
from jax import lax
from jax.experimental import pallas as pl
from jax.experimental.pallas import tpu as pltpu
from jax.sharding import PartitionSpec as P

PASSES = 16
STEPS = 4
GROUP = 8
HALO = 8
MESH = pl.DeviceIdType.MESH
BESIDE = (1, 3, 2)
F32 = jnp.float32
BF16 = jnp.bfloat16


def tables(columns):
    index = np.arange(1, columns + 1, dtype=np.float64)
    sine = np.sqrt(2.0 / (columns + 1)) * np.sin(np.pi * np.outer(index, index) / (columns + 1))
    high = sine.astype(BF16)
    low = (sine - high.astype(np.float64)).astype(BF16)
    center = (1.0 + 2.0 * np.cos(np.pi * index / (columns + 1))) / 5.0
    power = np.ones((1, columns))
    for _ in range(PASSES):
        wider = np.zeros((power.shape[0] + 2, columns))
        wider[1:-1] += center * power
        wider[2:] += power / 5.0
        wider[:-2] += power / 5.0
        power = wider
    coef = np.broadcast_to(power[PASSES:, None, :], (PASSES + 1, GROUP, columns))
    return high, low, np.ascontiguousarray(coef).astype(np.float32)


def split(x):
    high = x.astype(BF16)
    return high, (x - high.astype(F32)).astype(BF16)


def times_sine(x, vhi, vlo):
    high, low = split(x)
    out = jnp.dot(high, vhi[...], preferred_element_type=F32)
    out += jnp.dot(low, vhi[...], preferred_element_type=F32)
    out += jnp.dot(high, vlo[...], preferred_element_type=F32)
    return out


def kernel(
    regions, ctl, pert, assign, cour, innov, weight, vhi_in, vlo_in, coef_in,
    lft, dep_out,
    vhi, vlo, coef, ctl3, pbuf, sums, home, smo_out, smo, ms, inc, inc_far, cour_x, inn_x, wgt_x, adj, dep,
    modes, rows, mid, fin,
    load_sem, pert_send, pert_recv, z_send, z_recv, nb_send, nb_recv, pair_send, pair_recv,
    smo_send, smo_recv, fin_send, fin_recv, out_sem,
):
    r, me = lax.axis_index("region"), lax.axis_index("member")
    fl, levels, height, columns = ctl.shape
    kl = pert.shape[0]
    xs = levels // 2
    part_fields = fl * xs
    groups = 2 * part_fields // GROUP
    tiles = columns // 128
    last = regions - 1
    mx, mz = lax.rem(me, xs), me // xs
    beside = [x for x in BESIDE if x < xs]

    def at_x(x):
        return lax.rem(mx + x, xs)

    def beside_me(x):
        return mz * xs + at_x(x)

    across = (1 - mz) * xs + mx

    barrier = pltpu.get_barrier_semaphore()
    for x in beside:
        pl.semaphore_signal(barrier, inc=1, device_id=(r, beside_me(x)), device_id_type=MESH)
    pl.semaphore_signal(barrier, inc=1, device_id=(r, across), device_id_type=MESH)

    @pl.when(r > 0)
    def _():
        for to in (me, across):
            pl.semaphore_signal(barrier, inc=1, device_id=(r - 1, to), device_id_type=MESH)

    @pl.when(r < last)
    def _():
        for to in (me, across):
            pl.semaphore_signal(barrier, inc=1, device_id=(r + 1, to), device_id_type=MESH)

    loads = [
        pltpu.make_async_copy(vhi_in, vhi, load_sem.at[0]),
        pltpu.make_async_copy(vlo_in, vlo, load_sem.at[1]),
        pltpu.make_async_copy(coef_in, coef, load_sem.at[2]),
        pltpu.make_async_copy(ctl, ctl3.at[1], load_sem.at[3]),
        pltpu.make_async_copy(pert.at[:, mx], pbuf.at[0, pl.ds(mx * kl, kl)], load_sem.at[4]),
        pltpu.make_async_copy(pert.at[:, xs + mx], pbuf.at[1, pl.ds(mx * kl, kl)], load_sem.at[5]),
        pltpu.make_async_copy(cour.at[:, :, 0], cour_x.at[:, :, pl.ds(HALO, height)], load_sem.at[6]),
        pltpu.make_async_copy(innov.at[0], inn_x.at[pl.ds(HALO, height)], load_sem.at[7]),
        pltpu.make_async_copy(weight.at[0], wgt_x.at[pl.ds(HALO, height)], load_sem.at[8]),
    ]
    for copy in loads:
        copy.start()

    top, bottom = pl.ds(0, HALO), pl.ds(height - HALO, HALO)
    above, below = pl.ds(0, HALO), pl.ds(HALO + height, HALO)
    halves = (top, bottom)
    nb = [
        ((ctl, ctl3.at[0]), (ctl, ctl3.at[2]), me),
        ((cour.at[:, :, 0, bottom], cour_x.at[:, :, above]), (cour.at[:, :, 0, top], cour_x.at[:, :, below]), me),
        ((innov.at[0, bottom], inn_x.at[above]), (innov.at[0, top], inn_x.at[below]), me),
        ((weight.at[0, bottom], wgt_x.at[above]), (weight.at[0, top], wgt_x.at[below]), me),
        ((ms.at[1, :, :, top], ms.at[0, :, :, top]), (ms.at[1, :, :, top], ms.at[2, :, :, top]), me),
        ((ms.at[1, :, :, bottom], ms.at[0, :, :, bottom]), (ms.at[1, :, :, bottom], ms.at[2, :, :, bottom]), me),
        ((inc.at[0, pl.ds(height, HALO)], inc.at[0, above]), (inc.at[0, pl.ds(HALO, HALO)], inc.at[0, below]), me),
        ((inc_far.at[bottom], inc.at[1, above]), (inc_far.at[top], inc.at[1, below]), across),
        ((adj.at[mz, 1], adj.at[mz, 0]), (adj.at[mz, 1], adj.at[mz, 2]), me),
        ((adj.at[mz, 1], adj.at[mz, 0]), (adj.at[mz, 1], adj.at[mz, 2]), across),
    ]

    def to_neighbour(number, up):
        src, dst = nb[number][up]
        return pltpu.make_async_remote_copy(
            src_ref=src, dst_ref=dst, send_sem=nb_send.at[number, up], recv_sem=nb_recv.at[number, up],
            device_id=(r - 1 if up else r + 1, nb[number][2]), device_id_type=MESH,
        )

    def exchange(number):
        @pl.when(r < last)
        def _():
            to_neighbour(number, 0).start()

        @pl.when(r > 0)
        def _():
            to_neighbour(number, 1).start()

    def arrived(number):
        @pl.when(r > 0)
        def _():
            to_neighbour(number, 0).wait_recv()

        @pl.when(r < last)
        def _():
            to_neighbour(number, 1).wait_recv()

    def sent(number):
        @pl.when(r < last)
        def _():
            to_neighbour(number, 0).wait_send()

        @pl.when(r > 0)
        def _():
            to_neighbour(number, 1).wait_send()

    def pair_copy(number):
        src, dst = ((inc_far, inc.at[1, pl.ds(HALO, height)]), (adj.at[mz, 1], adj.at[mz, 1]))[number]
        return pltpu.make_async_remote_copy(
            src_ref=src, dst_ref=dst, send_sem=pair_send.at[number], recv_sem=pair_recv.at[number],
            device_id=(r, across), device_id_type=MESH,
        )

    def pert_copy(x, z, half):
        return pltpu.make_async_remote_copy(
            src_ref=pert.at[:, z * xs + at_x(x), halves[half]], dst_ref=pbuf.at[z, pl.ds(mx * kl, kl), halves[half]],
            send_sem=pert_send.at[x, z, half], recv_sem=pert_recv.at[x, z, half],
            device_id=(r, beside_me(x)), device_id_type=MESH,
        )

    def z_copy(z, half):
        return pltpu.make_async_remote_copy(
            src_ref=sums.at[z, pl.ds((1 - mz) * part_fields, part_fields), halves[half]],
            dst_ref=home.at[z, :, halves[half]],
            send_sem=z_send.at[z, half], recv_sem=z_recv.at[z, half],
            device_id=(r, across), device_id_type=MESH,
        )

    def smo_copy(x, field):
        return pltpu.make_async_remote_copy(
            src_ref=smo_out.at[field, :, at_x(x)], dst_ref=smo.at[:, mx * fl + field],
            send_sem=smo_send.at[x, field], recv_sem=smo_recv.at[x, field],
            device_id=(r, beside_me(x)), device_id_type=MESH,
        )

    def smo_own(field):
        return pltpu.make_async_copy(smo_out.at[field, :, mx], smo.at[:, mx * fl + field], smo_send.at[0, field])

    def fin_copy(x, z):
        return pltpu.make_async_remote_copy(
            src_ref=fin.at[x, z], dst_ref=lft.at[:, z * xs + mx],
            send_sem=fin_send.at[x, z], recv_sem=fin_recv.at[x, z],
            device_id=(r, beside_me(x)), device_id_type=MESH,
        )

    def fin_own(z):
        return pltpu.make_async_copy(fin.at[0, z], lft.at[:, z * xs + mx], fin_send.at[0, z])

    neighbours = (r > 0).astype(jnp.int32) + (r < last).astype(jnp.int32)
    pl.semaphore_wait(barrier, len(beside) + 1 + 2 * neighbours)

    exchange(0)
    pieces = [(z, half) for half in range(2) for z in range(2)]
    for z, half in pieces:
        for x in beside:
            pert_copy(x, z, half).start()
    for number in (1, 2, 3):
        exchange(number)

    @pl.when(r == 0)
    def _():
        for ref in (inn_x, wgt_x, inc.at[0], inc.at[1]):
            ref[0:HALO] = jnp.zeros((HALO, columns), F32)
        cour_x[:, :, 0:HALO] = jnp.zeros((STEPS, 4, HALO, columns), F32)

    @pl.when(r == last)
    def _():
        for ref in (inn_x, wgt_x, inc.at[0], inc.at[1]):
            ref[HALO + height :] = jnp.zeros((HALO, columns), F32)
        cour_x[:, :, HALO + height :] = jnp.zeros((STEPS, 4, HALO, columns), F32)

    def smooth(x):
        flat = jnp.concatenate([part.reshape(GROUP * height, columns) for part in x], axis=0)
        spectrum = times_sine(flat, vhi, vlo)
        for t in range(tiles):
            lane = slice(t * 128, (t + 1) * 128)
            modes[t] = spectrum[:, lane]
            for part in range(3):
                for i in range(height):
                    rows[part * height + i, :, lane] = modes[t, pl.ds(part * GROUP * height + i, GROUP, stride=height), :]

        @pl.when(r == 0)
        def _():
            rows[height - 1] = jnp.zeros((GROUP, columns), F32)
            for k in range(1, height):
                rows[height - 1 - k] = -rows[height - 1 + k]

        @pl.when(r == last)
        def _():
            rows[2 * height] = jnp.zeros((GROUP, columns), F32)
            for k in range(1, height):
                rows[2 * height + k] = -rows[2 * height - k]

        step = 4

        @pl.loop(0, tiles * (height // step))
        def _(it):
            t = lax.rem(it, tiles)
            lane = pl.ds(pl.multiple_of(t * 128, 128), 128)
            i = (it // tiles) * step
            g = [rows[i + j, :, lane] for j in range(2 * PASSES + step)]
            total = [None] * step
            for d in range(PASSES + 1):
                c = coef[d, :, lane]
                for j in range(step):
                    at = PASSES + j
                    term = c * g[at] if d == 0 else c * (g[at - d] + g[at + d])
                    total[j] = term if d == 0 else total[j] + term
            for j in range(step):
                mid[t, pl.ds(i + j, GROUP, stride=height), :] = total[j]

        result = times_sine(jnp.concatenate([mid[t] for t in range(tiles)], axis=1), vhi, vlo)
        return result.reshape(GROUP, height, columns)

    def add_source(x, z, half, first):
        which = [assign[(mz * xs + x) * kl + k] for k in range(kl)]
        p = [pbuf[z, x * kl + k, halves[half]] for k in range(kl)]
        for l in range(2 * part_fields):
            terms = [jnp.where(which[k] == l, 1.0, 0.0) * p[k] for k in range(kl)]
            while len(terms) > 1:
                terms = [a + b for a, b in zip(terms[::2], terms[1::2])]
            sums[z, l, halves[half]] = terms[0] if first else sums[z, l, halves[half]] + terms[0]

    def add_others(z, half):
        for x in beside:
            pert_copy(x, z, half).wait_recv()
            add_source(at_x(xs - x), z, half, False)
        z_copy(z, half).start()

    def finish(half):
        for z in range(2):
            z_copy(z, half).wait_recv()
            for l in range(part_fields):
                ms[1, z, l, halves[half]] = sums[z, mz * part_fields + l, halves[half]] + home[z, l, halves[half]]
        exchange(4 + half)

    loads[4].wait()
    loads[5].wait()
    for z, half in pieces:
        add_source(mx, z, half, True)
    for z, half in pieces[:2]:
        add_others(z, half)

    for number in range(4):
        loads[number].wait()
    arrived(0)
    for q in range(groups):
        planes = [((q * GROUP + j) // levels, (q * GROUP + j) % levels) for j in range(GROUP)]
        result = smooth([
            jnp.concatenate([ctl3[part, field, level][None] for field, level in planes]) for part in range(3)
        ])
        for j, (field, level) in enumerate(planes):
            smo_out[field, level // xs, level % xs] = result[j]
        for field in range(q * GROUP // levels, (q + 1) * GROUP // levels):
            for x in beside:
                smo_copy(x, field).start()
            smo_own(field).start()

    finish(0)
    for z, half in pieces[2:]:
        add_others(z, half)
    finish(1)

    for field in range(fl):
        smo_own(field).wait()
        for x in beside:
            smo_copy(x, field).wait_recv()

    def share(z):
        total = smo[z, 0] * ms[1, z, 0]
        for l in range(1, part_fields):
            total += smo[z, l] * ms[1, z, l]
        return total

    inc_far[...] = share(1 - mz)
    pair_copy(0).start()
    exchange(7)
    inc[0, HALO : HALO + height] = share(mz)
    exchange(6)
    for number in (6, 7, 8):
        loads[number].wait()
    for number in (1, 2, 3, 6, 7):
        arrived(number)
    pair_copy(0).wait_recv()

    extent = height + 2 * HALO
    column = lax.broadcasted_iota(jnp.int32, (extent, columns), 1)

    def from_west(y):
        return jnp.where(column == 0, 0.0, pltpu.roll(y, 1, 1))

    def from_east(y):
        return jnp.where(column == columns - 1, 0.0, pltpu.roll(y, columns - 1, 1))

    def from_north(y):
        return pltpu.roll(y, 1, 0)

    def from_south(y):
        return pltpu.roll(y, extent - 1, 0)

    state = inc[0] + inc[1]
    for s in range(STEPS):
        n, so, w, e = (cour_x[s, k] for k in range(4))
        state = (
            (1.0 - (n + so + w + e)) * state
            + n * from_north(state) + so * from_south(state) + w * from_west(state) + e * from_east(state)
        )
    state = wgt_x[...] * (state - inn_x[...])
    dep[...] = state[HALO : HALO + height]
    for s in range(STEPS - 1, -1, -1):
        n, so, w, e = (cour_x[s, k] for k in range(4))
        state = (
            (1.0 - (n + so + w + e)) * state
            + from_south(n * state) + from_north(so * state) + from_east(w * state) + from_west(e * state)
        )
    adj[mz, 1] = state[HALO : HALO + height]
    exchange(9)
    exchange(8)
    pair_copy(1).start()
    dep_copy = pltpu.make_async_copy(dep, dep_out.at[0], out_sem)
    dep_copy.start()

    def adj_arrived(up):
        far = 1 - mz
        return pltpu.make_async_remote_copy(
            src_ref=adj.at[far, 1], dst_ref=adj.at[far, 2 if up else 0],
            send_sem=nb_send.at[9, up], recv_sem=nb_recv.at[9, up],
            device_id=(r - 1 if up else r + 1, across), device_id_type=MESH,
        )

    for number in (4, 5, 8):
        arrived(number)

    @pl.when(r > 0)
    def _():
        adj_arrived(0).wait_recv()

    @pl.when(r < last)
    def _():
        adj_arrived(1).wait_recv()

    pltpu.make_async_remote_copy(
        src_ref=adj.at[1 - mz, 1], dst_ref=adj.at[1 - mz, 1], send_sem=pair_send.at[1], recv_sem=pair_recv.at[1],
        device_id=(r, across), device_id_type=MESH,
    ).wait_recv()

    owners = [x for x in (2, 1, 3, 0) if x < xs]
    per = GROUP // (2 * fl)
    for q in range(groups):
        mine = owners[q * per : (q + 1) * per]
        planes = [(x, z, f) for x in mine for z in range(2) for f in range(fl)]
        result = smooth([
            jnp.concatenate([(ms[part, z, at_x(x) * fl + f] * adj[z, part])[None] for x, z, f in planes])
            for part in range(3)
        ])
        for j, (x, z, f) in enumerate(planes):
            fin[x, z, f] = result[j]
        for x in mine:
            for z in range(2):
                if x:
                    fin_copy(x, z).start()
                else:
                    fin_own(z).start()

    for z, half in pieces:
        for x in beside:
            pert_copy(x, z, half).wait_send()
        z_copy(z, half).wait_send()
    for x in beside:
        for field in range(fl):
            smo_copy(x, field).wait_send()
    for number in range(len(nb)):
        sent(number)
    for number in range(2):
        pair_copy(number).wait_send()
    dep_copy.wait()
    for z in range(2):
        fin_own(z).wait()
        for x in beside:
            fin_copy(x, z).wait_send()
    for z in range(2):
        for x in beside:
            fin_copy(x, z).wait_recv()


def solution(mesh):
    regions = mesh.shape["region"]

    def shards(controls, perturbations, assignment, courant, innovation, obs_weight):
        fl, levels, height, columns = controls.shape
        kl = perturbations.shape[0]
        fields, xs = fl * levels, levels // 2
        vhi, vlo, coef = tables(columns)
        extent = height + 2 * HALO
        any_space = pl.BlockSpec(memory_space=pltpu.HBM)
        smem = pl.BlockSpec(memory_space=pltpu.SMEM)
        dma = pltpu.SemaphoreType.DMA
        lft, departure = pl.pallas_call(
            functools.partial(kernel, regions),
            out_shape=(
                jax.ShapeDtypeStruct(controls.shape, F32),
                jax.ShapeDtypeStruct(innovation.shape, F32),
            ),
            in_specs=[any_space, any_space, smem] + [any_space] * 6,
            out_specs=(any_space, any_space),
            scratch_shapes=[
                pltpu.VMEM((columns, columns), BF16),
                pltpu.VMEM((columns, columns), BF16),
                pltpu.VMEM((PASSES + 1, GROUP, columns), F32),
                pltpu.VMEM((3, fl, levels, height, columns), F32),
                pltpu.VMEM((2, kl * xs, height, columns), F32),
                pltpu.VMEM((2, fields, height, columns), F32),
                pltpu.VMEM((2, fl * xs, height, columns), F32),
                pltpu.VMEM((fl, 2, xs, height, columns), F32),
                pltpu.VMEM((2, fl * xs, height, columns), F32),
                pltpu.VMEM((3, 2, fl * xs, height, columns), F32),
                pltpu.VMEM((2, extent, columns), F32),
                pltpu.VMEM((height, columns), F32),
                pltpu.VMEM((STEPS, 4, extent, columns), F32),
                pltpu.VMEM((extent, columns), F32),
                pltpu.VMEM((extent, columns), F32),
                pltpu.VMEM((2, 3, height, columns), F32),
                pltpu.VMEM((height, columns), F32),
                pltpu.VMEM((columns // 128, 3 * GROUP * height, 128), F32),
                pltpu.VMEM((3 * height, GROUP, columns), F32),
                pltpu.VMEM((columns // 128, GROUP * height, 128), F32),
                pltpu.VMEM((xs, 2, fl, height, columns), F32),
                dma((9,)),
                dma((4, 2, 2)),
                dma((4, 2, 2)),
                dma((2, 2)),
                dma((2, 2)),
                dma((10, 2)),
                dma((10, 2)),
                dma((2,)),
                dma((2,)),
                dma((4, fl)),
                dma((4, fl)),
                dma((4, 2)),
                dma((4, 2)),
                dma,
            ],
            compiler_params=pltpu.CompilerParams(
                collective_id=0, has_side_effects=True, vmem_limit_bytes=56 * 2**20
            ),
            cost_estimate=pl.CostEstimate(flops=2 * 10**9, bytes_accessed=8 * 2**20, transcendentals=0),
        )(controls, perturbations, assignment, courant, innovation, obs_weight, vhi, vlo, coef)
        return controls + lft, departure

    return jax.shard_map(
        shards,
        mesh=mesh,
        in_specs=(
            P("member", None, "region", None),
            P("member", None, "region", None),
            P(),
            P(None, None, "member", "region", None),
            P("member", "region", None),
            P("member", "region", None),
        ),
        out_specs=(P("member", None, "region", None), P("member", "region", None)),
        check_vma=False,
    )
```

time: 72.2 us -> 62 us (0.86)
  Pallas kernels: 68 us -> 57.7 us
    pallas_call x1, Pallas kernels: 68 us -> 57.7 us  [shards(): pl.pallas_call(functools.partial(kernel, regions), out_shape=(jax.ShapeDt...]
where the time goes in v2:
time: 62 us; the launch traced here: 61.7 us
  Pallas kernels  57.7 us (93%)
  other arithmetic  1.93 us (3%)
  local copies, waits for them, and re-layouts  1.38 us (2%)
  between operations  0.66 us (1%)
    pallas_call x1, Pallas kernels, shards(): pl.pallas_call(functools.partial(kernel, regions), out_shape=(jax.ShapeDt...  57.7 us
    add x1, other arithmetic, shards(): return (controls + lft, departure)  1.93 us
    unnamed x3, local copies, waits for them, and re-layouts  1.38 us

profile of v2, /device:TPU:1, one launch (start us, length us, event | category | flops | bytes accessed | tf_op | source)
XLA Modules:
  0.0 61.7 jit_solution(11591986866987975967)
XLA Ops:
  0.6 0.0 copy-start
  0.6 57.7 %shard_map.104 = (f32[2,8,16,512]{3,2,1,0:T(8,128)}, f32[1,16,512]{2,1,0:T(8,128)}) custom-call(f32[2,8,16,512]{3,2,1,0:T(8,128)} %ctl.1, f32[8,8,16,512]{3,2,1,0:T(8,128)} %pert.1, s32[64]{0:T(128)} %assign.1, f32[4,4,1,16,512]{4,3,2,1,0:T(8,128)} %cour.1, f32[1,16,512]{2,1,0:T(8,128)} %innov.1, f32[1,16,512]{2,1,0:T(8,128)} %weight.1, ...), custom_call_target="tpu_custom_call" | custom-call | flops 2000000000 | bytes 8388608 | tf_op jit(solution)/shard_map/pallas_call | solution.py:448
  58.4 0.0 copy-done
  58.4 1.9 %add.3 = f32[2,8,16,512]{3,2,1,0:T(8,128)} add(f32[2,8,16,512]{3,2,1,0:T(8,128)S(1)} %copy-done, f32[2,8,16,512]{3,2,1,0:T(8,128)} %get-tuple-element.4) | non-fusion elementwise | flops 131072 | bytes 1572864 | tf_op jit(solution)/shard_map/add | solution.py:498
  60.3 1.4 %copy.12 = f32[1,16,512]{2,1,0:T(8,128)} copy(f32[1,16,512]{2,1,0:T(8,128)} %get-tuple-element.9) | data formatting | bytes 65536
Async XLA Ops:
  0.6 57.7 %copy-start = (f32[2,8,16,512]{3,2,1,0:T(8,128)S(1)}, f32[2,8,16,512]{3,2,1,0:T(8,128)}, u32[]{:S(2)}) copy-start(f32[2,8,16,512]{3,2,1,0:T(8,128)} %ctl.1) | copy-start | bytes 1572868

commit v3 on v2

--- a/solution.py
+++ b/solution.py
@@ -112,13 +112,16 @@
         ((cour.at[:, :, 0, bottom], cour_x.at[:, :, above]), (cour.at[:, :, 0, top], cour_x.at[:, :, below]), me),
         ((innov.at[0, bottom], inn_x.at[above]), (innov.at[0, top], inn_x.at[below]), me),
         ((weight.at[0, bottom], wgt_x.at[above]), (weight.at[0, top], wgt_x.at[below]), me),
-        ((ms.at[1, :, :, top], ms.at[0, :, :, top]), (ms.at[1, :, :, top], ms.at[2, :, :, top]), me),
-        ((ms.at[1, :, :, bottom], ms.at[0, :, :, bottom]), (ms.at[1, :, :, bottom], ms.at[2, :, :, bottom]), me),
         ((inc.at[0, pl.ds(height, HALO)], inc.at[0, above]), (inc.at[0, pl.ds(HALO, HALO)], inc.at[0, below]), me),
         ((inc_far.at[bottom], inc.at[1, above]), (inc_far.at[top], inc.at[1, below]), across),
         ((adj.at[mz, 1], adj.at[mz, 0]), (adj.at[mz, 1], adj.at[mz, 2]), me),
         ((adj.at[mz, 1], adj.at[mz, 0]), (adj.at[mz, 1], adj.at[mz, 2]), across),
     ]
+    pieces = [(z, half) for half in range(2) for z in range(2)]
+    first_piece = len(nb)
+    for z, half in pieces:
+        own = ms.at[1, z, :, halves[half]]
+        nb.append(((own, ms.at[0, z, :, halves[half]]), (own, ms.at[2, z, :, halves[half]]), me))
 
     def to_neighbour(number, up):
         src, dst = nb[number][up]
@@ -200,7 +203,6 @@
     pl.semaphore_wait(barrier, len(beside) + 1 + 2 * neighbours)
 
     exchange(0)
-    pieces = [(z, half) for half in range(2) for z in range(2)]
     for z, half in pieces:
         for x in beside:
             pert_copy(x, z, half).start()
@@ -220,14 +222,15 @@
         cour_x[:, :, HALO + height :] = jnp.zeros((STEPS, 4, HALO, columns), F32)
 
     def smooth(x):
-        flat = jnp.concatenate([part.reshape(GROUP * height, columns) for part in x], axis=0)
+        group = x[0].shape[0]
+        flat = jnp.concatenate([part.reshape(group * height, columns) for part in x], axis=0)
         spectrum = times_sine(flat, vhi, vlo)
         for t in range(tiles):
             lane = slice(t * 128, (t + 1) * 128)
-            modes[t] = spectrum[:, lane]
+            modes[t, : 3 * group * height] = spectrum[:, lane]
             for part in range(3):
                 for i in range(height):
-                    rows[part * height + i, :, lane] = modes[t, pl.ds(part * GROUP * height + i, GROUP, stride=height), :]
+                    rows[part * height + i, :group, lane] = modes[t, pl.ds(part * group * height + i, group, stride=height), :]
 
         @pl.when(r == 0)
         def _():
@@ -241,26 +244,26 @@
             for k in range(1, height):
                 rows[2 * height + k] = -rows[2 * height - k]
 
-        step = 4
+        step = 8
 
         @pl.loop(0, tiles * (height // step))
         def _(it):
             t = lax.rem(it, tiles)
             lane = pl.ds(pl.multiple_of(t * 128, 128), 128)
             i = (it // tiles) * step
-            g = [rows[i + j, :, lane] for j in range(2 * PASSES + step)]
+            g = [rows[i + j, :group, lane] for j in range(2 * PASSES + step)]
             total = [None] * step
             for d in range(PASSES + 1):
-                c = coef[d, :, lane]
+                c = coef[d, :group, lane]
                 for j in range(step):
                     at = PASSES + j
                     term = c * g[at] if d == 0 else c * (g[at - d] + g[at + d])
                     total[j] = term if d == 0 else total[j] + term
             for j in range(step):
-                mid[t, pl.ds(i + j, GROUP, stride=height), :] = total[j]
-
-        result = times_sine(jnp.concatenate([mid[t] for t in range(tiles)], axis=1), vhi, vlo)
-        return result.reshape(GROUP, height, columns)
+                mid[t, pl.ds(i + j, group, stride=height), :] = total[j]
+
+        own = jnp.concatenate([mid[t, : group * height] for t in range(tiles)], axis=1)
+        return times_sine(own, vhi, vlo).reshape(group, height, columns)
 
     def add_source(x, z, half, first):
         which = [assign[(mz * xs + x) * kl + k] for k in range(kl)]
@@ -277,12 +280,11 @@
             add_source(at_x(xs - x), z, half, False)
         z_copy(z, half).start()
 
-    def finish(half):
-        for z in range(2):
-            z_copy(z, half).wait_recv()
-            for l in range(part_fields):
-                ms[1, z, l, halves[half]] = sums[z, mz * part_fields + l, halves[half]] + home[z, l, halves[half]]
-        exchange(4 + half)
+    def finish(z, half):
+        z_copy(z, half).wait_recv()
+        for l in range(part_fields):
+            ms[1, z, l, halves[half]] = sums[z, mz * part_fields + l, halves[half]] + home[z, l, halves[half]]
+        exchange(first_piece + pieces.index((z, half)))
 
     loads[4].wait()
     loads[5].wait()
@@ -306,10 +308,12 @@
                 smo_copy(x, field).start()
             smo_own(field).start()
 
-    finish(0)
+    for z, half in pieces[:2]:
+        finish(z, half)
     for z, half in pieces[2:]:
         add_others(z, half)
-    finish(1)
+    for z, half in pieces[2:]:
+        finish(z, half)
 
     for field in range(fl):
         smo_own(field).wait()
@@ -324,12 +328,12 @@
 
     inc_far[...] = share(1 - mz)
     pair_copy(0).start()
-    exchange(7)
+    exchange(5)
     inc[0, HALO : HALO + height] = share(mz)
-    exchange(6)
+    exchange(4)
     for number in (6, 7, 8):
         loads[number].wait()
-    for number in (1, 2, 3, 6, 7):
+    for number in (1, 2, 3, 4, 5):
         arrived(number)
     pair_copy(0).wait_recv()
 
@@ -364,8 +368,8 @@
             + from_south(n * state) + from_north(so * state) + from_east(w * state) + from_west(e * state)
         )
     adj[mz, 1] = state[HALO : HALO + height]
-    exchange(9)
-    exchange(8)
+    exchange(7)
+    exchange(6)
     pair_copy(1).start()
     dep_copy = pltpu.make_async_copy(dep, dep_out.at[0], out_sem)
     dep_copy.start()
@@ -374,11 +378,11 @@
         far = 1 - mz
         return pltpu.make_async_remote_copy(
             src_ref=adj.at[far, 1], dst_ref=adj.at[far, 2 if up else 0],
-            send_sem=nb_send.at[9, up], recv_sem=nb_recv.at[9, up],
+            send_sem=nb_send.at[7, up], recv_sem=nb_recv.at[7, up],
             device_id=(r - 1 if up else r + 1, across), device_id_type=MESH,
         )
 
-    for number in (4, 5, 8):
+    for number in [*range(first_piece, len(nb)), 6]:
         arrived(number)
 
     @pl.when(r > 0)
@@ -394,10 +398,10 @@
         device_id=(r, across), device_id_type=MESH,
     ).wait_recv()
 
-    owners = [x for x in (2, 1, 3, 0) if x < xs]
-    per = GROUP // (2 * fl)
-    for q in range(groups):
-        mine = owners[q * per : (q + 1) * per]
+    for mine in ((2,), (1, 3), (0,)):
+        mine = [x for x in mine if x < xs]
+        if not mine:
+            continue
         planes = [(x, z, f) for x in mine for z in range(2) for f in range(fl)]
         result = smooth([
             jnp.concatenate([(ms[part, z, at_x(x) * fl + f] * adj[z, part])[None] for x, z, f in planes])
@@ -480,8 +484,8 @@
                 dma((4, 2, 2)),
                 dma((2, 2)),
                 dma((2, 2)),
-                dma((10, 2)),
-                dma((10, 2)),
+                dma((12, 2)),
+                dma((12, 2)),
                 dma((2,)),
                 dma((2,)),
                 dma((4, fl)),

time: 62 us -> 60.8 us (0.981); the launches traced: 61.7 us -> 59.6 us
  Pallas kernels: 57.7 us -> 55.7 us
    pallas_call x1, Pallas kernels: 57.7 us -> 55.7 us  [shards(): pl.pallas_call(functools.partial(kernel, regions), out_shape=(jax.ShapeDt...]
where the time goes in v3:
time: 60.8 us; the launch traced here: 59.6 us
  Pallas kernels  55.7 us (92%)
  other arithmetic  1.93 us (3%)
  local copies, waits for them, and re-layouts  1.38 us (2%)
  between operations  0.66 us (1%)
    pallas_call x1, Pallas kernels, shards(): pl.pallas_call(functools.partial(kernel, regions), out_shape=(jax.ShapeDt...  55.7 us
    add x1, other arithmetic, shards(): return (controls + lft, departure)  1.93 us
    unnamed x3, local copies, waits for them, and re-layouts  1.38 us

profile of v3, /device:TPU:1, one launch (start us, length us, event | category | flops | bytes accessed | tf_op | source)
XLA Modules:
  0.0 59.6 jit_solution(378967660484957055)
XLA Ops:
  0.6 0.0 copy-start
  0.6 55.7 %shard_map.104 = (f32[2,8,16,512]{3,2,1,0:T(8,128)}, f32[1,16,512]{2,1,0:T(8,128)}) custom-call(f32[2,8,16,512]{3,2,1,0:T(8,128)} %ctl.1, f32[8,8,16,512]{3,2,1,0:T(8,128)} %pert.1, s32[64]{0:T(128)} %assign.1, f32[4,4,1,16,512]{4,3,2,1,0:T(8,128)} %cour.1, f32[1,16,512]{2,1,0:T(8,128)} %innov.1, f32[1,16,512]{2,1,0:T(8,128)} %weight.1, ...), custom_call_target="tpu_custom_call" | custom-call | flops 2000000000 | bytes 8388608 | tf_op jit(solution)/shard_map/pallas_call | solution.py:452
  56.3 0.0 copy-done
  56.3 1.9 %add.3 = f32[2,8,16,512]{3,2,1,0:T(8,128)} add(f32[2,8,16,512]{3,2,1,0:T(8,128)S(1)} %copy-done, f32[2,8,16,512]{3,2,1,0:T(8,128)} %get-tuple-element.4) | non-fusion elementwise | flops 131072 | bytes 1572864 | tf_op jit(solution)/shard_map/add | solution.py:502
  58.2 1.4 %copy.12 = f32[1,16,512]{2,1,0:T(8,128)} copy(f32[1,16,512]{2,1,0:T(8,128)} %get-tuple-element.9) | data formatting | bytes 65536
Async XLA Ops:
  0.6 55.7 %copy-start = (f32[2,8,16,512]{3,2,1,0:T(8,128)S(1)}, f32[2,8,16,512]{3,2,1,0:T(8,128)}, u32[]{:S(2)}) copy-start(f32[2,8,16,512]{3,2,1,0:T(8,128)} %ctl.1) | copy-start | bytes 1572868

commit v4 on v3

--- a/solution.py
+++ b/solution.py
@@ -446,17 +446,17 @@
         fields, xs = fl * levels, levels // 2
         vhi, vlo, coef = tables(columns)
         extent = height + 2 * HALO
-        any_space = pl.BlockSpec(memory_space=pltpu.HBM)
+        in_hbm = pl.BlockSpec(memory_space=pltpu.HBM)
         smem = pl.BlockSpec(memory_space=pltpu.SMEM)
         dma = pltpu.SemaphoreType.DMA
         lft, departure = pl.pallas_call(
             functools.partial(kernel, regions),
             out_shape=(
-                jax.ShapeDtypeStruct(controls.shape, F32),
-                jax.ShapeDtypeStruct(innovation.shape, F32),
+                pltpu.VMEM(controls.shape, F32),
+                pltpu.VMEM(innovation.shape, F32),
             ),
-            in_specs=[any_space, any_space, smem] + [any_space] * 6,
-            out_specs=(any_space, any_space),
+            in_specs=[in_hbm, in_hbm, smem] + [in_hbm] * 6,
+            out_specs=(pl.BlockSpec(memory_space=pl.ANY),) * 2,
             scratch_shapes=[
                 pltpu.VMEM((columns, columns), BF16),
                 pltpu.VMEM((columns, columns), BF16),

time: 60.8 us -> 58.8 us (0.967)
  other arithmetic: 1.93 us -> 0.88 us
  local copies, waits for them, and re-layouts: 1.38 us -> 0.62 us
    add x1, other arithmetic: 1.93 us -> 0.88 us  [shards(): return (controls + lft, departure)]
    unnamed x3, local copies, waits for them, and re-layouts: 1.38 us -> 0.62 us
where the time goes in v4:
time: 58.8 us; the launch traced here: 57.7 us
  Pallas kernels  55.6 us (95%)
  other arithmetic  0.88 us (1%)
  between operations  0.66 us (1%)
  local copies, waits for them, and re-layouts  0.62 us (1%)
    pallas_call x1, Pallas kernels, shards(): pl.pallas_call(functools.partial(kernel, regions), out_shape=(pltpu.VMEM(...  55.6 us

profile of v4, /device:TPU:1, one launch (start us, length us, event | category | flops | bytes accessed | tf_op | source)
XLA Modules:
  0.0 57.7 jit_solution(9052152642844328206)
XLA Ops:
  0.6 0.0 copy-start
  0.6 55.6 %shard_map.104 = (f32[2,8,16,512]{3,2,1,0:T(8,128)S(1)}, f32[1,16,512]{2,1,0:T(8,128)S(1)}) custom-call(f32[2,8,16,512]{3,2,1,0:T(8,128)} %ctl.1, f32[8,8,16,512]{3,2,1,0:T(8,128)} %pert.1, s32[64]{0:T(128)} %assign.1, f32[4,4,1,16,512]{4,3,2,1,0:T(8,128)} %cour.1, f32[1,16,512]{2,1,0:T(8,128)} %innov.1, f32[1,16,512]{2,1,0:T(8,128)} %weight.1, ...), custom_call_target="tpu_custom_call" | custom-call | flops 2000000000 | bytes 8388608 | tf_op jit(solution)/shard_map/pallas_call | solution.py:452
  56.2 0.0 copy-done
  56.2 0.9 %add.3 = f32[2,8,16,512]{3,2,1,0:T(8,128)} add(f32[2,8,16,512]{3,2,1,0:T(8,128)S(1)} %copy-done, f32[2,8,16,512]{3,2,1,0:T(8,128)S(1)} %get-tuple-element.4) | non-fusion elementwise | flops 131072 | bytes 1572864 | tf_op jit(solution)/shard_map/add | solution.py:502
  57.1 0.6 %copy.12 = f32[1,16,512]{2,1,0:T(8,128)} copy(f32[1,16,512]{2,1,0:T(8,128)S(1)} %get-tuple-element.7) | data formatting | bytes 65536
Async XLA Ops:
  0.6 55.6 %copy-start = (f32[2,8,16,512]{3,2,1,0:T(8,128)S(1)}, f32[2,8,16,512]{3,2,1,0:T(8,128)}, u32[]{:S(2)}) copy-start(f32[2,8,16,512]{3,2,1,0:T(8,128)} %ctl.1) | copy-start | bytes 1572868

commit v5 on v4

--- a/solution.py
+++ b/solution.py
@@ -117,7 +117,7 @@
         ((adj.at[mz, 1], adj.at[mz, 0]), (adj.at[mz, 1], adj.at[mz, 2]), me),
         ((adj.at[mz, 1], adj.at[mz, 0]), (adj.at[mz, 1], adj.at[mz, 2]), across),
     ]
-    pieces = [(z, half) for half in range(2) for z in range(2)]
+    pieces = [(z, half) for z in range(2) for half in range(2)]
     first_piece = len(nb)
     for z, half in pieces:
         own = ms.at[1, z, :, halves[half]]
@@ -179,15 +179,20 @@
             device_id=(r, across), device_id_type=MESH,
         )
 
-    def smo_copy(x, field):
-        return pltpu.make_async_remote_copy(
-            src_ref=smo_out.at[field, :, at_x(x)], dst_ref=smo.at[:, mx * fl + field],
-            send_sem=smo_send.at[x, field], recv_sem=smo_recv.at[x, field],
+    def smo_copy(x, field, z):
+        return pltpu.make_async_remote_copy(
+            src_ref=smo_out.at[field, z, at_x(x)], dst_ref=smo.at[z, mx * fl + field],
+            send_sem=smo_send.at[x, field, z], recv_sem=smo_recv.at[x, field, z],
             device_id=(r, beside_me(x)), device_id_type=MESH,
         )
 
-    def smo_own(field):
-        return pltpu.make_async_copy(smo_out.at[field, :, mx], smo.at[:, mx * fl + field], smo_send.at[0, field])
+    def smo_own(field, z):
+        return pltpu.make_async_copy(smo_out.at[field, z, mx], smo.at[z, mx * fl + field], smo_send.at[0, field, z])
+
+    def send_smoothed(field, z):
+        for x in beside:
+            smo_copy(x, field, z).start()
+        smo_own(field, z).start()
 
     def fin_copy(x, z):
         return pltpu.make_async_remote_copy(
@@ -203,9 +208,12 @@
     pl.semaphore_wait(barrier, len(beside) + 1 + 2 * neighbours)
 
     exchange(0)
-    for z, half in pieces:
+    def send_piece(z, half):
         for x in beside:
             pert_copy(x, z, half).start()
+
+    for z, half in pieces[:2]:
+        send_piece(z, half)
     for number in (1, 2, 3):
         exchange(number)
 
@@ -290,8 +298,8 @@
     loads[5].wait()
     for z, half in pieces:
         add_source(mx, z, half, True)
-    for z, half in pieces[:2]:
-        add_others(z, half)
+    add_others(0, 0)
+    send_piece(1, 0)
 
     for number in range(4):
         loads[number].wait()
@@ -304,38 +312,30 @@
         for j, (field, level) in enumerate(planes):
             smo_out[field, level // xs, level % xs] = result[j]
         for field in range(q * GROUP // levels, (q + 1) * GROUP // levels):
+            send_smoothed(field, 0)
+    send_piece(1, 1)
+    for field in range(fl):
+        send_smoothed(field, 1)
+
+    def increment(z):
+        for field in range(fl):
+            smo_own(field, z).wait()
             for x in beside:
-                smo_copy(x, field).start()
-            smo_own(field).start()
-
-    for z, half in pieces[:2]:
-        finish(z, half)
-    for z, half in pieces[2:]:
-        add_others(z, half)
-    for z, half in pieces[2:]:
-        finish(z, half)
-
-    for field in range(fl):
-        smo_own(field).wait()
-        for x in beside:
-            smo_copy(x, field).wait_recv()
-
-    def share(z):
+                smo_copy(x, field, z).wait_recv()
         total = smo[z, 0] * ms[1, z, 0]
         for l in range(1, part_fields):
             total += smo[z, l] * ms[1, z, l]
-        return total
-
-    inc_far[...] = share(1 - mz)
-    pair_copy(0).start()
-    exchange(5)
-    inc[0, HALO : HALO + height] = share(mz)
-    exchange(4)
-    for number in (6, 7, 8):
-        loads[number].wait()
-    for number in (1, 2, 3, 4, 5):
-        arrived(number)
-    pair_copy(0).wait_recv()
+
+        @pl.when(mz == z)
+        def _():
+            inc[0, HALO : HALO + height] = total
+            exchange(4)
+
+        @pl.when(mz != z)
+        def _():
+            inc_far[...] = total
+            pair_copy(0).start()
+            exchange(5)
 
     extent = height + 2 * HALO
     column = lax.broadcasted_iota(jnp.int32, (extent, columns), 1)
@@ -352,27 +352,34 @@
     def from_south(y):
         return pltpu.roll(y, extent - 1, 0)
 
-    state = inc[0] + inc[1]
-    for s in range(STEPS):
-        n, so, w, e = (cour_x[s, k] for k in range(4))
-        state = (
-            (1.0 - (n + so + w + e)) * state
-            + n * from_north(state) + so * from_south(state) + w * from_west(state) + e * from_east(state)
-        )
-    state = wgt_x[...] * (state - inn_x[...])
-    dep[...] = state[HALO : HALO + height]
-    for s in range(STEPS - 1, -1, -1):
-        n, so, w, e = (cour_x[s, k] for k in range(4))
-        state = (
-            (1.0 - (n + so + w + e)) * state
-            + from_south(n * state) + from_north(so * state) + from_east(w * state) + from_west(e * state)
-        )
-    adj[mz, 1] = state[HALO : HALO + height]
-    exchange(7)
-    exchange(6)
-    pair_copy(1).start()
     dep_copy = pltpu.make_async_copy(dep, dep_out.at[0], out_sem)
-    dep_copy.start()
+
+    def transport():
+        for number in (6, 7, 8):
+            loads[number].wait()
+        for number in (1, 2, 3, 4, 5):
+            arrived(number)
+        pair_copy(0).wait_recv()
+        state = inc[0] + inc[1]
+        for s in range(STEPS):
+            n, so, w, e = (cour_x[s, k] for k in range(4))
+            state = (
+                (1.0 - (n + so + w + e)) * state
+                + n * from_north(state) + so * from_south(state) + w * from_west(state) + e * from_east(state)
+            )
+        state = wgt_x[...] * (state - inn_x[...])
+        dep[...] = state[HALO : HALO + height]
+        for s in range(STEPS - 1, -1, -1):
+            n, so, w, e = (cour_x[s, k] for k in range(4))
+            state = (
+                (1.0 - (n + so + w + e)) * state
+                + from_south(n * state) + from_north(so * state) + from_east(w * state) + from_west(e * state)
+            )
+        adj[mz, 1] = state[HALO : HALO + height]
+        exchange(7)
+        exchange(6)
+        pair_copy(1).start()
+        dep_copy.start()
 
     def adj_arrived(up):
         far = 1 - mz
@@ -382,39 +389,60 @@
             device_id=(r - 1 if up else r + 1, across), device_id_type=MESH,
         )
 
-    for number in [*range(first_piece, len(nb)), 6]:
-        arrived(number)
-
-    @pl.when(r > 0)
-    def _():
-        adj_arrived(0).wait_recv()
-
-    @pl.when(r < last)
-    def _():
-        adj_arrived(1).wait_recv()
-
-    pltpu.make_async_remote_copy(
-        src_ref=adj.at[1 - mz, 1], dst_ref=adj.at[1 - mz, 1], send_sem=pair_send.at[1], recv_sem=pair_recv.at[1],
-        device_id=(r, across), device_id_type=MESH,
-    ).wait_recv()
-
-    for mine in ((2,), (1, 3), (0,)):
-        mine = [x for x in mine if x < xs]
-        if not mine:
-            continue
-        planes = [(x, z, f) for x in mine for z in range(2) for f in range(fl)]
-        result = smooth([
-            jnp.concatenate([(ms[part, z, at_x(x) * fl + f] * adj[z, part])[None] for x, z, f in planes])
-            for part in range(3)
-        ])
-        for j, (x, z, f) in enumerate(planes):
-            fin[x, z, f] = result[j]
-        for x in mine:
-            for z in range(2):
+    def adj_pair_arrived():
+        return pltpu.make_async_remote_copy(
+            src_ref=adj.at[1 - mz, 1], dst_ref=adj.at[1 - mz, 1], send_sem=pair_send.at[1], recv_sem=pair_recv.at[1],
+            device_id=(r, across), device_id_type=MESH,
+        )
+
+    def second(z, chunks):
+        for half in range(2):
+            arrived(first_piece + pieces.index((z, half)))
+
+        @pl.when(mz == z)
+        def _():
+            arrived(6)
+
+        @pl.when(mz != z)
+        def _():
+            @pl.when(r > 0)
+            def _():
+                adj_arrived(0).wait_recv()
+
+            @pl.when(r < last)
+            def _():
+                adj_arrived(1).wait_recv()
+
+            adj_pair_arrived().wait_recv()
+
+        for mine in chunks:
+            mine = [x for x in mine if x < xs]
+            planes = [(x, f) for x in mine for f in range(fl)]
+            result = smooth([
+                jnp.concatenate([(ms[part, z, at_x(x) * fl + f] * adj[z, part])[None] for x, f in planes])
+                for part in range(3)
+            ])
+            for j, (x, f) in enumerate(planes):
+                fin[x, z, f] = result[j]
+            for x in mine:
                 if x:
                     fin_copy(x, z).start()
                 else:
                     fin_own(z).start()
+
+    add_others(0, 1)
+    finish(0, 0)
+    finish(0, 1)
+    add_others(1, 0)
+    increment(0)
+    finish(1, 0)
+    add_others(1, 1)
+    finish(1, 1)
+    increment(1)
+    pl.when(mz == 0)(transport)
+    pl.when(mz == 1)(transport)
+    second(0, ((2, 1, 3, 0),))
+    second(1, ((2, 1, 3, 0),))
 
     for z, half in pieces:
         for x in beside:
@@ -422,7 +450,8 @@
         z_copy(z, half).wait_send()
     for x in beside:
         for field in range(fl):
-            smo_copy(x, field).wait_send()
+            for z in range(2):
+                smo_copy(x, field, z).wait_send()
     for number in range(len(nb)):
         sent(number)
     for number in range(2):
@@ -488,8 +517,8 @@
                 dma((12, 2)),
                 dma((2,)),
                 dma((2,)),
-                dma((4, fl)),
-                dma((4, fl)),
+                dma((4, fl, 2)),
+                dma((4, fl, 2)),
                 dma((4, 2)),
                 dma((4, 2)),
                 dma,

time: 58.8 us -> 58.2 us (0.990)
  no operation moved by 1% of the time
where the time goes in v5:
time: 58.2 us; the launch traced here: 57.6 us
  Pallas kernels  55.4 us (95%)
  other arithmetic  0.88 us (2%)
  between operations  0.66 us (1%)
  local copies, waits for them, and re-layouts  0.62 us (1%)
    pallas_call x1, Pallas kernels, shards(): pl.pallas_call(functools.partial(kernel, regions), out_shape=(pltpu.VMEM(...  55.4 us

profile of v5, /device:TPU:1, one launch (start us, length us, event | category | flops | bytes accessed | tf_op | source)
XLA Modules:
  0.0 57.6 jit_solution(4831608088252821753)
XLA Ops:
  0.6 0.0 copy-start
  0.6 55.4 %shard_map.104 = (f32[2,8,16,512]{3,2,1,0:T(8,128)S(1)}, f32[1,16,512]{2,1,0:T(8,128)S(1)}) custom-call(f32[2,8,16,512]{3,2,1,0:T(8,128)} %ctl.1, f32[8,8,16,512]{3,2,1,0:T(8,128)} %pert.1, s32[64]{0:T(128)} %assign.1, f32[4,4,1,16,512]{4,3,2,1,0:T(8,128)} %cour.1, f32[1,16,512]{2,1,0:T(8,128)} %innov.1, f32[1,16,512]{2,1,0:T(8,128)} %weight.1, ...), custom_call_target="tpu_custom_call" | custom-call | flops 2000000000 | bytes 8388608 | tf_op jit(solution)/shard_map/pallas_call | solution.py:481
  56.1 0.0 copy-done
  56.1 0.9 %add.3 = f32[2,8,16,512]{3,2,1,0:T(8,128)} add(f32[2,8,16,512]{3,2,1,0:T(8,128)S(1)} %copy-done, f32[2,8,16,512]{3,2,1,0:T(8,128)S(1)} %get-tuple-element.4) | non-fusion elementwise | flops 131072 | bytes 1572864 | tf_op jit(solution)/shard_map/add | solution.py:531
  57.0 0.6 %copy.12 = f32[1,16,512]{2,1,0:T(8,128)} copy(f32[1,16,512]{2,1,0:T(8,128)S(1)} %get-tuple-element.7) | data formatting | bytes 65536
Async XLA Ops:
  0.6 55.5 %copy-start = (f32[2,8,16,512]{3,2,1,0:T(8,128)S(1)}, f32[2,8,16,512]{3,2,1,0:T(8,128)}, u32[]{:S(2)}) copy-start(f32[2,8,16,512]{3,2,1,0:T(8,128)} %ctl.1) | copy-start | bytes 1572868

commit v6 on v5

--- a/solution.py
+++ b/solution.py
@@ -318,13 +318,15 @@
         send_smoothed(field, 1)
 
     def increment(z):
-        for field in range(fl):
-            smo_own(field, z).wait()
-            for x in beside:
-                smo_copy(x, field, z).wait_recv()
-        total = smo[z, 0] * ms[1, z, 0]
-        for l in range(1, part_fields):
-            total += smo[z, l] * ms[1, z, l]
+        total = jnp.zeros((height, columns), F32)
+        for x in (0, *beside):
+            for field in range(fl):
+                if x:
+                    smo_copy(x, field, z).wait_recv()
+                else:
+                    smo_own(field, z).wait()
+                l = at_x(xs - x) * fl + field
+                total += smo[z, l] * ms[1, z, l]
 
         @pl.when(mz == z)
         def _():
@@ -439,8 +441,7 @@
     add_others(1, 1)
     finish(1, 1)
     increment(1)
-    pl.when(mz == 0)(transport)
-    pl.when(mz == 1)(transport)
+    transport()
     second(0, ((2, 1, 3, 0),))
     second(1, ((2, 1, 3, 0),))
 

time: 58.2 us -> 58.2 us (level)
  no operation moved by 1% of the time
where the time goes in v6:
time: 58.2 us; the launch traced here: 57.6 us
  Pallas kernels  55.4 us (95%)
  other arithmetic  0.88 us (2%)
  between operations  0.66 us (1%)
  local copies, waits for them, and re-layouts  0.62 us (1%)
    pallas_call x1, Pallas kernels, shards(): pl.pallas_call(functools.partial(kernel, regions), out_shape=(pltpu.VMEM(...  55.4 us

profile of v6, /device:TPU:1, one launch (start us, length us, event | category | flops | bytes accessed | tf_op | source)
XLA Modules:
  0.0 57.6 jit_solution(15943829045621517899)
XLA Ops:
  0.6 0.0 copy-start
  0.6 55.4 %shard_map.104 = (f32[2,8,16,512]{3,2,1,0:T(8,128)S(1)}, f32[1,16,512]{2,1,0:T(8,128)S(1)}) custom-call(f32[2,8,16,512]{3,2,1,0:T(8,128)} %ctl.1, f32[8,8,16,512]{3,2,1,0:T(8,128)} %pert.1, s32[64]{0:T(128)} %assign.1, f32[4,4,1,16,512]{4,3,2,1,0:T(8,128)} %cour.1, f32[1,16,512]{2,1,0:T(8,128)} %innov.1, f32[1,16,512]{2,1,0:T(8,128)} %weight.1, ...), custom_call_target="tpu_custom_call" | custom-call | flops 2000000000 | bytes 8388608 | tf_op jit(solution)/shard_map/pallas_call | solution.py:482
  56.1 0.0 copy-done
  56.1 0.9 %add.3 = f32[2,8,16,512]{3,2,1,0:T(8,128)} add(f32[2,8,16,512]{3,2,1,0:T(8,128)S(1)} %copy-done, f32[2,8,16,512]{3,2,1,0:T(8,128)S(1)} %get-tuple-element.4) | non-fusion elementwise | flops 131072 | bytes 1572864 | tf_op jit(solution)/shard_map/add | solution.py:532
  57.0 0.6 %copy.12 = f32[1,16,512]{2,1,0:T(8,128)} copy(f32[1,16,512]{2,1,0:T(8,128)S(1)} %get-tuple-element.7) | data formatting | bytes 65536
Async XLA Ops:
  0.6 55.5 %copy-start = (f32[2,8,16,512]{3,2,1,0:T(8,128)S(1)}, f32[2,8,16,512]{3,2,1,0:T(8,128)}, u32[]{:S(2)}) copy-start(f32[2,8,16,512]{3,2,1,0:T(8,128)} %ctl.1) | copy-start | bytes 1572868
